TPU v7x, 32 devices: a whole 2x2x4 slice. The times are simulated.
32 devices in a mesh: seq: 4 (over z), tp: 8 (over y, x, core).
Axes of the slice: x: 2, y: 2, z: 4, core: 2. Of those that a mesh axis runs over, the one named last changes fastest.
Arguments:
- patch_tokens: bfloat16 [2, 4096, 1024], P(None, 'seq'), may hold values from -6 to 6
- plane_tokens: bfloat16 [2, 3072, 1024], P(None, 'seq'), may hold values from -6 to 6
- norm1_gain: float32 [1024], replicated, may hold values from 0.5 to 1.5
- norm1_bias: float32 [1024], replicated, may hold values from -1 to 1
- w_query: bfloat16 [1024, 1024], P(None, 'tp'), may hold values from -0.375 to 0.375
- w_key: bfloat16 [1024, 1024], P(None, 'tp'), may hold values from -0.1875 to 0.1875
- w_value: bfloat16 [1024, 1024], P(None, 'tp'), may hold values from -0.1875 to 0.1875
- w_out: bfloat16 [1024, 1024], P('tp'), may hold values from -2 to 2
- norm2_gain: float32 [1024], replicated, may hold values from 0.5 to 1.5
- norm2_bias: float32 [1024], replicated, may hold values from -1 to 1
- w_up: bfloat16 [1024, 4096], P(None, 'tp'), may hold values from -0.1875 to 0.1875
- w_down: bfloat16 [4096, 1024], P('tp'), may hold values from -0.09375 to 0.09375
- w_unpatch: bfloat16 [1024, 2048], P(None, 'tp'), may hold values from -0.1875 to 0.1875
- b_unpatch: float32 [2048], P('tp'), may hold values from -3 to 3
- w_dec1: float32 [32, 64], replicated, may hold values from -1 to 1
- b_dec1: float32 [64], replicated, may hold values from -3 to 3
- w_dec2: float32 [64, 4], replicated, may hold values from -0.75 to 0.75
- tile_index: int32 [2, 3, 128], P(None, None, 'seq'), may hold values from 0 to 1023
- corner_weights: bfloat16 [2, 128, 3, 64, 128], P(None, 'seq', None, 'tp'), may hold values from 0 to 1, as said below
- ray_count: int32 [2], replicated, may hold values from 32 to 128, as said below
- color_grad: float32 [2, 3, 128], P(None, None, ('seq', 'tp')), may hold values from -6 to 6
Outputs:
- colors: float32 [2, 3, 128], P(None, None, ('seq', 'tp'))
- patch_grad: float32 [2, 4096, 1024], P(None, ('seq', 'tp'))
- plane_grad: float32 [2, 3072, 1024], P(None, ('seq', 'tp'))
- norm1_gain_grad: float32 [1024], P('tp')
- norm1_bias_grad: float32 [1024], P('tp')
- query_grad: float32 [1024, 1024], P(None, 'tp')
- key_grad: float32 [1024, 1024], P(None, 'tp')
- value_grad: float32 [1024, 1024], P(None, 'tp')
- out_weight_grad: float32 [1024, 1024], P('tp')
- norm2_gain_grad: float32 [1024], P('tp')
- norm2_bias_grad: float32 [1024], P('tp')
- up_grad: float32 [1024, 4096], P(None, 'tp')
- down_grad: float32 [4096, 1024], P('tp')
- unpatch_grad: float32 [1024, 2048], P(None, 'tp')
- unpatch_bias_grad: float32 [2048], P('tp')
- dec1_grad: float32 [32, 64], P(None, 'tp')
- dec1_bias_grad: float32 [64], P('tp')
- dec2_grad: float32 [64, 4], P('tp')
Inputs may be any that keep to these rules, and one draw needn't show every extreme that they name: Scene n's live rays are its first ray_count[n] ray slots; the later slots are padding. Some scene has all 128 slots live. `corner_weights`: for each ray, plane and sample, the column over the 64 pixels holds the bilinear weights of one point inside the 8 by 8 tile: nonnegative, at most four nonzero, summing to one.
All inputs are finite; a program needn't handle non-finite values.
Results may differ from a plain program's by a relative error of at most 0.023.
Values may be sent and summed in bfloat16 or wider, within the bound.
No kernel may reach another device: no remote copies, remote signals or barrier semaphores. Data moves between devices by JAX's collectives and lax.ppermute only.
A program may use at most 448 MiB of HBM per device.

v0:
```python
import jax
import jax.numpy as jnp
from jax import lax
from jax.sharding import PartitionSpec as P

HEAD_DIM = 64
CH = 32
TRI_SIDE = 32


def norm_rows(token_rows, norm_gain, norm_shift):
    centre = jnp.mean(token_rows, axis=-1, keepdims=True)
    offset = token_rows - centre
    spread = jnp.mean(offset * offset, axis=-1, keepdims=True)
    return offset * lax.rsqrt(spread + 1e-05) * norm_gain + norm_shift


def render(features, dec_first, dec_bias, dec_second, live_rays):
    preact = (
        jnp.einsum("ch,...cs->...hs", dec_first, features, precision=lax.Precision.HIGHEST)
        + dec_bias[:, None]
    )
    hidden = jax.nn.silu(preact)
    output = jnp.einsum("hk,...hs->...ks", dec_second, hidden, precision=lax.Precision.HIGHEST)
    density = jax.nn.softplus(output[..., 0, :])
    colour = jax.nn.sigmoid(output[..., 1:, :])
    optical = density * (2.0 / output.shape[-1])
    through = jnp.exp(-(jnp.cumsum(optical, axis=-1) - optical))
    weight = through * (1.0 - jnp.exp(-optical))
    return jnp.sum(weight[..., None, :] * colour, axis=-1) * live_rays[..., None]


def collect_keys(key_value):
    return lax.all_gather(key_value, "seq", axis=1, tiled=True)


def head_views(queries, key_value):
    head_count = queries.shape[-1] // HEAD_DIM
    split_at = head_count * HEAD_DIM
    query_heads = queries.reshape(queries.shape[0], head_count, HEAD_DIM)
    key_heads = key_value[:, :split_at].reshape(key_value.shape[0], head_count, HEAD_DIM)
    value_heads = key_value[:, split_at:].reshape(key_value.shape[0], head_count, HEAD_DIM)
    return (query_heads, key_heads, value_heads)


def attend_scene(scene_data):
    queries, key_value = scene_data
    query_heads, key_heads, value_heads = head_views(queries, key_value)
    scores = jnp.einsum(
        "qhd,khd->hqk", query_heads, key_heads, preferred_element_type=jnp.float32
    ) * HEAD_DIM ** (-0.5)
    row_max = jnp.max(scores, axis=-1, keepdims=True)
    raised = jnp.exp(scores - row_max)
    row_total = jnp.sum(raised, axis=-1, keepdims=True)
    shares = (raised / row_total).astype(jnp.bfloat16)
    mixed = jnp.einsum("hqk,khd->qhd", shares, value_heads, preferred_element_type=jnp.float32)
    return (
        mixed.reshape(queries.shape[0], queries.shape[1]),
        (row_max + jnp.log(row_total))[..., 0],
    )


def score_grads(query_heads, key_heads, value_heads, grad_heads, logsum, inner_sum):
    scores = jnp.einsum(
        "qhd,khd->hqk", query_heads, key_heads, preferred_element_type=jnp.float32
    ) * HEAD_DIM ** (-0.5)
    shares = jnp.exp(scores - logsum[..., None])
    grad_shares = jnp.einsum(
        "qhd,khd->hqk", grad_heads, value_heads, preferred_element_type=jnp.float32
    )
    inner_sum = jnp.sum(shares * grad_shares, axis=-1)
    grad_scores = (shares * (grad_shares - inner_sum[..., None])).astype(
        jnp.bfloat16
    ) * jnp.bfloat16(HEAD_DIM ** (-0.5))
    return (shares, grad_scores, inner_sum)


def key_side(shares, grad_scores, query_heads, grad_heads, key_rows):
    grad_key = jnp.einsum(
        "hqk,qhd->khd", grad_scores, query_heads, preferred_element_type=jnp.float32
    )
    grad_value = jnp.einsum(
        "hqk,qhd->khd", shares.astype(jnp.bfloat16), grad_heads, preferred_element_type=jnp.float32
    )
    return jnp.concatenate(
        [grad_key.reshape(key_rows, -1), grad_value.reshape(key_rows, -1)], axis=-1
    )


def attend_back(scene_data):
    queries, key_value, grad_mixed, logsum = scene_data
    query_heads, key_heads, value_heads = head_views(queries, key_value)
    grad_heads = grad_mixed.reshape(query_heads.shape)
    shares, grad_scores, inner_sum = score_grads(
        query_heads, key_heads, value_heads, grad_heads, logsum, None
    )
    grad_query = jnp.einsum(
        "hqk,khd->qhd", grad_scores, key_heads, preferred_element_type=jnp.float32
    )
    return (
        grad_query.reshape(queries.shape),
        key_side(shares, grad_scores, query_heads, grad_heads, key_value.shape[0]),
    )


def on_device(
    patch_tokens,
    plane_tokens,
    norm1_gain,
    norm1_bias,
    w_query,
    w_key,
    w_value,
    w_out,
    norm2_gain,
    norm2_bias,
    w_up,
    w_down,
    w_unpatch,
    b_unpatch,
    w_dec1,
    b_dec1,
    w_dec2,
    tile_index,
    corner_weights,
    ray_count,
    color_grad,
):
    scenes = patch_tokens.shape[0]
    patch_local = patch_tokens.shape[1]
    plane_local = plane_tokens.shape[1]
    tp_count = lax.axis_size("tp")
    tp_rank = lax.axis_index("tp")
    own_patch = patch_local // tp_count
    own_plane = plane_local // tp_count
    rows_in = jnp.concatenate([patch_tokens, plane_tokens], axis=1).astype(jnp.float32)
    normed = norm_rows(rows_in, norm1_gain, norm1_bias).astype(jnp.bfloat16)
    plane_normed = normed[:, patch_local:]
    queries = jnp.einsum(
        "nrd,de->nre", plane_normed, w_query, preferred_element_type=jnp.float32
    ).astype(jnp.bfloat16)
    key_weight = jnp.concatenate([w_key, w_value], axis=1)
    key_value = jnp.einsum(
        "nrd,de->nre", normed, key_weight, preferred_element_type=jnp.float32
    ).astype(jnp.bfloat16)
    gathered = collect_keys(key_value)
    mixed, logsum = lax.map(attend_scene, (queries, gathered))
    mixed_low = mixed.astype(jnp.bfloat16)
    branch = lax.psum(
        jnp.einsum("nqe,ed->nqd", mixed_low, w_out, preferred_element_type=jnp.float32), "tp"
    )
    hidden_state = rows_in[:, patch_local:] + branch
    normed2 = norm_rows(hidden_state, norm2_gain, norm2_bias).astype(jnp.bfloat16)
    preact = jnp.einsum("nrd,df->nrf", normed2, w_up, preferred_element_type=jnp.float32)
    active = jax.nn.gelu(preact).astype(jnp.bfloat16)
    result = hidden_state + lax.psum(
        jnp.einsum("nrf,fd->nrd", active, w_down, preferred_element_type=jnp.float32), "tp"
    )
    result_low = result.astype(jnp.bfloat16)
    tile_block = (
        jnp.einsum("nrd,dc->rnc", result_low, w_unpatch, preferred_element_type=jnp.float32)
        + b_unpatch
    ).astype(jnp.bfloat16)
    tile_cols = tile_block.shape[2]
    plane_base = (jnp.arange(3, dtype=jnp.int32) * (TRI_SIDE * TRI_SIDE))[None, :, None]
    tile_ids = (tile_index + plane_base).reshape(scenes, -1)
    scene_ids = jnp.broadcast_to(jnp.arange(scenes, dtype=jnp.int32)[:, None], tile_ids.shape)
    portion = lax.all_gather(tile_block, "seq", axis=0, tiled=True)
    relative = tile_ids
    inside = (relative >= 0) & (relative < portion.shape[0])
    fetched = portion[jnp.clip(relative, 0, portion.shape[0] - 1), scene_ids]
    picked = jnp.where(inside[..., None], fetched, jnp.zeros_like(fetched))
    pixel_local = tile_cols // CH
    picked = picked.reshape(scenes, 3, -1, pixel_local, CH)
    partial_value = jnp.einsum(
        "nprxc,nrpxs->nrcs", picked, corner_weights, preferred_element_type=jnp.float32
    )
    features = lax.psum_scatter(partial_value, "tp", scatter_dimension=1, tiled=True)
    ray_local = features.shape[1]
    first_ray = (lax.axis_index("seq") * tp_count + tp_rank) * ray_local
    live_rays = (
        (first_ray + jnp.arange(ray_local, dtype=jnp.int32))[None, :] < ray_count[:, None]
    ).astype(jnp.float32)

    def draw_colours(feature_rows, dec_first, dec_bias, dec_second):
        return render(feature_rows, dec_first, dec_bias, dec_second, live_rays)

    colours, pullback = jax.vjp(draw_colours, features, w_dec1, b_dec1, w_dec2)
    grad_features, dec1_part, dec1_bias_part, dec2_part = pullback(jnp.moveaxis(color_grad, 1, -1))
    feature_grads = lax.all_gather(grad_features, "tp", axis=1, tiled=True)
    grad_picked = jnp.einsum(
        "nrcs,nrpxs->nprxc",
        feature_grads,
        corner_weights.astype(jnp.float32),
        precision=lax.Precision.HIGHEST,
    ).reshape(scenes, -1, tile_cols)
    row_count = tile_block.shape[0] * lax.axis_size("seq")
    relative = tile_ids
    inside = (relative >= 0) & (relative < row_count)
    target = jnp.where(inside, relative, row_count)
    grad_tiles = lax.psum_scatter(
        jnp.zeros((row_count, scenes, tile_cols), jnp.float32)
        .at[target, scene_ids]
        .add(grad_picked, mode="drop"),
        "seq",
        scatter_dimension=0,
        tiled=True,
    ).astype(jnp.bfloat16)
    unpatch_part = jnp.einsum(
        "nrd,rnc->dc", result_low, grad_tiles, preferred_element_type=jnp.float32
    )
    unpatch_bias_part = jnp.sum(grad_tiles.astype(jnp.float32), axis=(0, 1))
    grad_result = lax.psum_scatter(
        jnp.einsum("rnc,dc->nrd", grad_tiles, w_unpatch, preferred_element_type=jnp.float32),
        "tp",
        scatter_dimension=1,
        tiled=True,
    )
    result_rows = lax.all_gather(grad_result.astype(jnp.bfloat16), "tp", axis=1, tiled=True)
    down_part = jnp.einsum("nrf,nrd->fd", active, result_rows, preferred_element_type=jnp.float32)
    grad_active = jnp.einsum("nrd,fd->nrf", result_rows, w_down, preferred_element_type=jnp.float32)
    grad_preact = jax.vjp(jax.nn.gelu, preact)[1](grad_active)[0].astype(jnp.bfloat16)
    up_part = jnp.einsum("nrd,nrf->df", normed2, grad_preact, preferred_element_type=jnp.float32)
    grad_normed2 = lax.psum_scatter(
        jnp.einsum("nrf,df->nrd", grad_preact, w_up, preferred_element_type=jnp.float32),
        "tp",
        scatter_dimension=1,
        tiled=True,
    )
    hidden_own = lax.dynamic_slice_in_dim(hidden_state, tp_rank * own_plane, own_plane, 1)
    norm2_pull = jax.vjp(norm_rows, hidden_own, norm2_gain, norm2_bias)[1]
    grad_hidden_norm, gain2_part, shift2_part = norm2_pull(grad_normed2)
    grad_hidden = grad_result + grad_hidden_norm
    hidden_rows = lax.all_gather(grad_hidden.astype(jnp.bfloat16), "tp", axis=1, tiled=True)
    out_part = jnp.einsum("nqe,nqd->ed", mixed_low, hidden_rows, preferred_element_type=jnp.float32)
    grad_mixed = jnp.einsum(
        "nqd,ed->nqe", hidden_rows, w_out, preferred_element_type=jnp.float32
    ).astype(jnp.bfloat16)
    delayed, _ = lax.optimization_barrier((key_value, grad_mixed))
    keys_again = collect_keys(delayed)
    grad_query, grad_kv = lax.map(attend_back, (queries, keys_again, grad_mixed, logsum))
    grad_kv = lax.psum_scatter(grad_kv, "seq", scatter_dimension=1, tiled=True).astype(jnp.bfloat16)
    grad_query = grad_query.astype(jnp.bfloat16)
    query_part = jnp.einsum(
        "nrd,nre->de", plane_normed, grad_query, preferred_element_type=jnp.float32
    )
    kv_part = jnp.einsum("nrd,nre->de", normed, grad_kv, preferred_element_type=jnp.float32)
    key_cols = w_key.shape[1]
    grad_normed = jnp.einsum("nre,de->nrd", grad_kv, key_weight, preferred_element_type=jnp.float32)
    patch_part = grad_normed[:, :patch_local]
    plane_part = grad_normed[:, patch_local:] + jnp.einsum(
        "nre,de->nrd", grad_query, w_query, preferred_element_type=jnp.float32
    )
    standard = norm_rows(rows_in, 1.0, 0.0)
    gain1_part = jnp.sum(patch_part * standard[:, :patch_local], axis=(0, 1)) + jnp.sum(
        plane_part * standard[:, patch_local:], axis=(0, 1)
    )
    shift1_part = jnp.sum(patch_part, axis=(0, 1)) + jnp.sum(plane_part, axis=(0, 1))
    reduced = (
        lax.psum_scatter(patch_part, "tp", scatter_dimension=1, tiled=True),
        lax.psum_scatter(plane_part, "tp", scatter_dimension=1, tiled=True),
        lax.psum_scatter(gain1_part, "tp", scatter_dimension=0, tiled=True),
        lax.psum_scatter(shift1_part, "tp", scatter_dimension=0, tiled=True),
        lax.psum_scatter(gain2_part, "tp", scatter_dimension=0, tiled=True),
        lax.psum_scatter(shift2_part, "tp", scatter_dimension=0, tiled=True),
        lax.psum_scatter(dec1_part, "tp", scatter_dimension=1, tiled=True),
        lax.psum_scatter(dec1_bias_part, "tp", scatter_dimension=0, tiled=True),
        lax.psum_scatter(dec2_part, "tp", scatter_dimension=0, tiled=True),
    )

    def norm_only(token_rows):
        return norm_rows(token_rows, norm1_gain, norm1_bias)

    patch_own = lax.dynamic_slice_in_dim(
        rows_in[:, :patch_local], tp_rank * own_patch, own_patch, 1
    )
    plane_own = lax.dynamic_slice_in_dim(
        rows_in[:, patch_local:], tp_rank * own_plane, own_plane, 1
    )
    patch_grad = jax.vjp(norm_only, patch_own)[1](reduced[0])[0]
    plane_grad = jax.vjp(norm_only, plane_own)[1](reduced[1])[0] + grad_hidden
    summed = lax.psum(
        (
            query_part,
            kv_part[:, :key_cols],
            kv_part[:, key_cols:],
            out_part,
            up_part,
            down_part,
            unpatch_part,
            unpatch_bias_part,
            reduced[2],
            reduced[3],
            reduced[4],
            reduced[5],
            reduced[6],
            reduced[7],
            reduced[8],
        ),
        "seq",
    )
    colours_out = jnp.moveaxis(colours, -1, 1)
    return (
        colours_out,
        patch_grad,
        plane_grad,
        summed[8],
        summed[9],
        summed[0],
        summed[1],
        summed[2],
        summed[3],
        summed[10],
        summed[11],
        summed[4],
        summed[5],
        summed[6],
        summed[7],
        summed[12],
        summed[13],
        summed[14],
    )


def solution(mesh):
    in_specs = (
        P(None, "seq", None),
        P(None, "seq", None),
        P(),
        P(),
        P(None, "tp"),
        P(None, "tp"),
        P(None, "tp"),
        P("tp", None),
        P(),
        P(),
        P(None, "tp"),
        P("tp", None),
        P(None, "tp"),
        P("tp"),
        P(),
        P(),
        P(),
        P(None, None, "seq"),
        P(None, "seq", None, "tp", None),
        P(),
        P(None, None, ("seq", "tp")),
    )
    out_specs = (
        P(None, None, ("seq", "tp")),
        P(None, ("seq", "tp"), None),
        P(None, ("seq", "tp"), None),
        P("tp"),
        P("tp"),
        P(None, "tp"),
        P(None, "tp"),
        P(None, "tp"),
        P("tp", None),
        P("tp"),
        P("tp"),
        P(None, "tp"),
        P("tp", None),
        P(None, "tp"),
        P("tp"),
        P(None, "tp"),
        P("tp"),
        P("tp", None),
    )
    return jax.shard_map(
        on_device, mesh=mesh, in_specs=in_specs, out_specs=out_specs, check_vma=False
    )
```

profile of v0, /device:TPU:0, one launch (start us, length us, event | category | flops | bytes accessed | tf_op | source)
XLA Modules:
  0.0 2310.3 jit_solution(16175218317408767259)
XLA Ops:
  17.1 7.8 subtract_multiply_fusion
  34.7 132.0 %all-gather.7.cloned.1.call-done = bf16[2,7168,256]{2,1,0:T(8,128)(2,1)} async-done(((bf16[2,1792,256]{2,1,0:T(8,128)(2,1)}), bf16[2,7168,256]{2,1,0:T(8,128)(2,1)}) %all-gather.7.cloned.1.call-update) | async-done | bytes 7340048 | tf_op jit(solution)/shard_map/all_gather | solution.py:34
  166.8 121.4 %while.24 = (s32[]{:T(128)}, bf16[2,768,128]{1,2,0:T(8,128)(2,1)S(1)}, f32[2,2,768]{2,1,0:T(2,128)S(1)}, bf16[2,7168,256]{2,1,0:T(8,128)(2,1)}, bf16[2,768,128]{1,2,0:T(8,128)(2,1)S(1)}, /*index=5*/s32[]{:T(128)}) while((s32[]{:T(128)}, bf16[2,768,128]{1,2,0:T(8,128)(2,1)S(1)}, f32[2,2,768]{2,1,0:T(2,128)S(1)}, ...), condition=%wide.region_5.6_spmd, body=%wide.region_2.5_spmd.sunk | while | flops 2917661184 | bytes 159039584 | solution.py:147
  170.9 5.9 copy.137
  179.1 17.1 multiply_reduce_fusion.14
  196.1 14.6 fusion.178
  210.7 16.7 fusion.179
  239.7 17.1 multiply_reduce_fusion.14
  256.8 14.6 fusion.178
  271.4 16.7 fusion.179
  292.2 10.3 fusion.112
  302.5 91.9 %all-reduce.20.cloned.1.call-done = f32[2,768,1024]{2,1,0:T(8,128)} async-done(((f32[2,768,1024]{2,1,0:T(8,128)}), f32[2,768,1024]{2,1,0:T(8,128)}) %all-reduce.20.cloned.1.call-update) | async-done | bytes 6291472 | tf_op jit(solution)/shard_map/psum | solution.py:149
  394.4 10.1 fusion.116
  417.7 104.3 %all-reduce.22.cloned.1.call-done = f32[2,768,1024]{2,1,0:T(8,128)} async-done(((f32[2,768,1024]{2,1,0:T(8,128)}), f32[2,768,1024]{2,1,0:T(8,128)}) %all-reduce.22.cloned.1.call-update) | async-done | bytes 6291472 | tf_op jit(solution)/shard_map/psum | solution.py:156
  532.3 62.8 %all-gather.9.cloned.1.call-done = bf16[3072,2,256]{2,0,1:T(8,128)(2,1)} async-done(((bf16[768,2,256]{2,0,1:T(8,128)(2,1)}), bf16[3072,2,256]{2,0,1:T(8,128)(2,1)}) %all-gather.9.cloned.1.call-update) | async-done | bytes 3145744 | tf_op jit(solution)/shard_map/all_gather | solution.py:168
  595.1 7.9 copy.86
  610.2 53.8 %all-reduce.24.cloned.1.call-done = f32[2,32,32,128]{3,2,1,0:T(8,128)} async-done(((f32[2,32,32,128]{3,2,1,0:T(8,128)}), f32[2,32,32,128]{3,2,1,0:T(8,128)}) %all-reduce.24.cloned.1.call-update) | async-done | bytes 1048592
  669.0 10.1 reduce_window_sum.23
  682.7 21.3 all-gather.11.cloned.1.call-done
  710.7 20.8 scatter_fusion
  731.4 218.1 %all-reduce.27 = bf16[3072,2,256]{2,1,0:T(2,128)(2,1)} all-reduce(f32[3072,2,256]{2,1,0:T(2,128)} %scatter_fusion), channel_id=3, replica_groups=mesh['seq'=4,'tp'=8] {'seq'}, use_global_device_ids=true, to_apply=%region_16.17.clone | all-reduce | flops 1572864 | bytes 9437184
  957.6 59.8 %reduce-scatter.10.cloned.1.call-done = f32[2,96,1024]{2,1,0:T(8,128)} async-done(((f32[2,768,1024]{2,1,0:T(8,128)}), f32[2,96,1024]{2,1,0:T(8,128)}) %reduce-scatter.10.cloned.1.call-update) | async-done | bytes 786448 | tf_op jit(solution)/shard_map/reduce_scatter | solution.py:213
  1019.4 33.0 %all-gather.13.cloned.1.call-done = bf16[2,768,1024]{2,1,0:T(8,128)(2,1)} async-done(((bf16[2,96,1024]{2,1,0:T(8,128)(2,1)}), bf16[2,768,1024]{2,1,0:T(8,128)(2,1)}) %all-gather.13.cloned.1.call-update) | async-done | bytes 3145744 | tf_op jit(solution)/shard_map/all_gather | solution.py:219
  1052.4 5.9 fusion.31
  1066.7 59.1 %reduce-scatter.12.cloned.1.call-done = f32[2,96,1024]{2,1,0:T(8,128)} async-done(((f32[2,768,1024]{2,1,0:T(8,128)}), f32[2,96,1024]{2,1,0:T(8,128)}) %reduce-scatter.12.cloned.1.call-update) | async-done | bytes 786448 | tf_op jit(solution)/shard_map/reduce_scatter | solution.py:224
  1131.7 32.4 %all-gather.15.cloned.1.call-done = bf16[2,768,1024]{2,1,0:T(8,128)(2,1)} async-done(((bf16[2,96,1024]{2,1,0:T(8,128)(2,1)}), bf16[2,768,1024]{2,1,0:T(8,128)(2,1)}) %all-gather.15.cloned.1.call-update) | async-done | bytes 3145744 | tf_op jit(solution)/shard_map/all_gather | solution.py:234
  1167.0 132.6 %all-gather.17.cloned.1.call-done = bf16[2,7168,256]{2,1,0:T(8,128)(2,1)} async-done(((bf16[2,1792,256]{2,1,0:T(8,128)(2,1)}), bf16[2,7168,256]{2,1,0:T(8,128)(2,1)}) %all-gather.17.cloned.1.call-update) | async-done | bytes 7340048 | tf_op jit(solution)/shard_map/all_gather | solution.py:34
  1300.4 330.4 %while.25 = (s32[]{:T(128)}, bf16[2,768,128]{1,2,0:T(8,128)(2,1)}, f32[2,7168,256]{1,2,0:T(8,128)}, bf16[2,7168,256]{2,1,0:T(8,128)(2,1)}, bf16[2,768,128]{1,2,0...) while((s32[]{:T(128)}, bf16[2,768,128]{1,2,0:T(8,128)(2,1)}, ...), condition=%wide.region_25.26_spmd, body=%wide.region_23.25_spmd.sunk | while | flops 7191405056 | bytes 356212928 | solution.py:241
  1313.2 17.0 fusion.192
  1330.2 17.0 fusion.193
  1347.3 70.0 %multiply_convert_fusion.5 = bf16[2,768,7168]{2,1,0:T(8,128)(2,1)} fusion(f32[2,768,7168]{2,1,0:T(8,128)} %fusion.192, f32[2,768,7168]{2,1,0:T(8,128)} %fusion.193, f32[2,768]{1,0:T(2,128)S(1)} %dynamic-slice_bitcast_fusion.2), kind=kOutput, calls=%fused_computation.13.clone.1 | output fusion | flops 88089088 | bytes 110106624 | tf_op jit(solution)/shard_map/while/body/eval_jaxpr/sub | solution.py:72
  1417.2 18.5 fusion.195
  1435.7 11.1 fusion.194
  1446.8 13.2 fusion.196
  1478.2 17.0 fusion.192
  1495.2 17.0 fusion.193
  1512.2 70.0 %multiply_convert_fusion.5 = bf16[2,768,7168]{2,1,0:T(8,128)(2,1)} fusion(f32[2,768,7168]{2,1,0:T(8,128)} %fusion.192, f32[2,768,7168]{2,1,0:T(8,128)} %fusion.193, f32[2,768]{1,0:T(2,128)S(1)} %dynamic-slice_bitcast_fusion.2), kind=kOutput, calls=%fused_computation.13.clone.1 | output fusion | flops 88089088 | bytes 110106624 | tf_op jit(solution)/shard_map/while/body/eval_jaxpr/sub | solution.py:72
  1582.2 18.5 fusion.195
  1600.7 11.1 fusion.194
  1611.8 13.2 fusion.196
  1631.0 244.0 %reduce-scatter.14.cloned.1.call-done = f32[2,1792,256]{1,2,0:T(8,128)} async-done(((f32[2,7168,256]{1,2,0:T(8,128)}), f32[2,1792,256]{1,2,0:T(8,128)}) %reduce-scatter.14.cloned.1.call-update) | async-done | bytes 3670032 | tf_op jit(solution)/shard_map/reduce_scatter | solution.py:242
  1879.1 10.0 fusion.113
  1889.2 10.4 slice_reduce_fusion
  1921.2 8.5 slice.70
  1936.5 25.0 %all-reduce.11 = (f32[1024]{0:T(1024)S(1)}, f32[1024]{0:T(1024)S(1)}, f32[1024]{0:T(1024)S(1)}, f32[1024]{0:T(1024)S(1)}, f32[32,64]{0,1:T(8,128)S(1)}, /*index=5*/f32[64]{0:T(128)S(1)}, f32[64,4]{0,1:T(4,128)S(1)}) all-reduce(f32[1024]{0:T(1024)S(1)} %add.314, f32[1024]{0:T(1024)S(1)} %add.315, ...), channel_id=9, replica_groups=mesh['seq'=4,'tp'=8] {'tp'}, use_global_device_ids=true, to_apply=%region_39.40.clone | all-reduce | flops 6464 | bytes 51712
  1961.9 12.9 all-reduce.12
  1980.8 46.8 %reduce-scatter.16.cloned.1.call-done = f32[2,128,1024]{2,1,0:T(8,128)} async-done(((f32[2,1024,1024]{2,1,0:T(8,128)}), f32[2,128,1024]{2,1,0:T(8,128)}) %reduce-scatter.16.cloned.1.call-update) | async-done | bytes 1048592 | tf_op jit(solution)/shard_map/reduce_scatter | solution.py:260
  2034.3 256.1 %all-reduce.26.cloned.1.call-done = (f32[1024,128]{1,0:T(8,128)}, f32[1024,128]{1,0:T(8,128)}, f32[1024,128]{1,0:T(8,128)}, f32[128,1024]{1,0:T(8,128)}, f32[102...) async-done(((f32[1024,128]{1,0:T(8,128)}, f32[1024,128]{1,0:T(8,128)}, f32[1024,128]{1,0:T(8,128)}, f32[128,1024]{1,0:T(8,128)}, f32[1024,512]{1,0:T(8,128)}, ...) | async-done | bytes 7340048 | tf_op jit(solution)/shard_map/psum | solution.py:282
  (338 shorter events, 207.9 us)
Async XLA Ops:
  7.2 405.7 %copy-start = (bf16[512,1024]{1,0:T(8,128)(2,1)S(1)}, bf16[512,1024]{1,0:T(8,128)(2,1)}, u32[]{:S(2)}) copy-start(bf16[512,1024]{1,0:T(8,128)(2,1)} %param.36) | copy-start | bytes 3145732
  7.2 159.5 %all-gather.7.cloned.1.call-start = ((), (), s32[]{:S(2)}) async-start(), calls=%async_computation.5 | async-start | bytes 9175040 | tf_op jit(solution)/shard_map/all_gather | solution.py:34
  31.4 363.0 %all-reduce.20.cloned.1.call-start = ((), (), s32[]{:S(2)}) async-start(), calls=%async_computation.6 | async-start | bytes 12582912 | tf_op jit(solution)/shard_map/psum | solution.py:149
  166.7 121.4 %copy-start.29 = (bf16[128,1024]{1,0:T(8,128)(2,1)S(1)}, bf16[128,1024]{1,0:T(8,128)(2,1)}, u32[]{:S(2)}) copy-start(bf16[128,1024]{1,0:T(8,128)(2,1)} %param.32) | copy-start | bytes 786436
  291.9 230.2 %all-reduce.22.cloned.1.call-start = ((), (), s32[]{:S(2)}) async-start(), calls=%async_computation.7 | async-start | bytes 12582912 | tf_op jit(solution)/shard_map/psum | solution.py:156
  417.6 111.8 %copy-start.30 = (bf16[1024,256]{1,0:T(8,128)(2,1)S(1)}, bf16[1024,256]{1,0:T(8,128)(2,1)}, u32[]{:S(2)}) copy-start(bf16[1024,256]{1,0:T(8,128)(2,1)} %param.37) | copy-start | bytes 1572868
  417.6 111.8 %copy-start.71 = (f32[256]{0:T(256)S(1)}, f32[256]{0:T(256)}, u32[]{:S(2)}) copy-start(f32[256]{0:T(256)} %param.38) | copy-start | bytes 3076
  417.6 177.4 %all-gather.9.cloned.1.call-start = ((), (), s32[]{:S(2)}) async-start(), calls=%async_computation.8 | async-start | bytes 3932160 | tf_op jit(solution)/shard_map/all_gather | solution.py:168
  529.4 77.6 %copy-start.20 = (bf16[2,32,3,8,128]{4,3,2,1,0:T(8,128)(2,1)S(1)}, bf16[2,32,3,8,128]{4,3,2,1,0:T(8,128)(2,1)}, u32[]{:S(2)}) copy-start(bf16[2,32,3,8,128]{4,3,2,1,0:T(8,128)(2,1)} %param.43) | copy-start | bytes 1179652
  531.3 77.5 %copy-start.64 = (s32[2]{0:T(128)S(1)}, s32[2]{0:T(128)}, u32[]{:S(2)}) copy-start(s32[2]{0:T(128)} %param.44) | copy-start | bytes 28
  531.3 77.5 %copy-start.61 = (f32[2,3,4]{2,0,1:T(2,128)S(1)}, f32[2,3,4]{2,0,1:T(2,128)}, u32[]{:S(2)}) copy-start(f32[2,3,4]{2,0,1:T(2,128)} %param.45) | copy-start | bytes 292
  531.3 77.7 %copy-start.73 = (u32[32]{0:T(128)S(1)}, u32[32]{0:T(128)}, u32[]{:S(2)}) copy-start(u32[32]{0:T(128)} %constant.171) | copy-start | bytes 388
  531.3 132.7 %copy-start.41 = (f32[32,64]{1,0:T(8,128)S(1)}, f32[32,64]{1,0:T(8,128)}, u32[]{:S(2)}) copy-start(f32[32,64]{1,0:T(8,128)} %param.39) | copy-start | bytes 24580
  531.3 132.7 %copy-start.63 = (f32[64]{0:T(128)S(1)}, f32[64]{0:T(128)}, u32[]{:S(2)}) copy-start(f32[64]{0:T(128)} %param.40) | copy-start | bytes 772
  531.3 134.0 %copy-start.70 = (f32[64,4]{0,1:T(4,128)S(1)}, f32[64,4]{0,1:T(4,128)}, u32[]{:S(2)}) copy-start(f32[64,4]{0,1:T(4,128)} %param.41) | copy-start | bytes 3076
  531.4 132.7 %all-reduce.24.cloned.1.call-start = ((), (), s32[]{:S(2)}) async-start(), calls=%async_computation.18 | async-start | bytes 2097152
  532.3 149.0 %copy-start.72 = (u32[32]{0:T(128)S(1)}, u32[32]{0:T(128)}, u32[]{:S(2)}) copy-start(u32[32]{0:T(128)} %constant.175) | copy-start | bytes 388
  608.7 95.3 %all-gather.11.cloned.1.call-start = ((), (), s32[]{:S(2)}) async-start(), calls=%async_computation.9 | async-start | bytes 1179648 | tf_op jit(solution)/shard_map/all_gather | solution.py:190
  608.9 59.3 %copy-start.53 = (f32[2,4]{1,0:T(2,128)}, f32[2,4]{1,0:T(2,128)S(1)}, u32[]{:S(2)}) copy-start(f32[2,4]{1,0:T(2,128)S(1)} %compare_convert_fusion) | copy-start | bytes 100
  665.4 38.6 %copy-start.24 = (f32[2,4,128,64]{2,3,1,0:T(8,128)}, f32[2,4,128,64]{2,3,1,0:T(8,128)S(1)}, u32[]{:S(2)}) copy-start(f32[2,4,128,64]{2,3,1,0:T(8,128)S(1)} %convolution_add_fusion) | copy-start | bytes 786436
  668.3 42.4 %copy-start.48 = (f32[2,4,3,128]{3,2,1,0:T(4,128)}, f32[2,4,3,128]{3,2,1,0:T(4,128)S(1)}, u32[]{:S(2)}) copy-start(f32[2,4,3,128]{3,2,1,0:T(4,128)S(1)} %get-tuple-element.207) | copy-start | bytes 36868
  679.1 27.0 %copy-start.59 = (f32[2,4,1,128]{3,2,1,0:T(1,128)}, f32[2,4,1,128]{3,2,1,0:T(1,128)S(1)}, u32[]{:S(2)}) copy-start(f32[2,4,1,128]{3,2,1,0:T(1,128)S(1)} %exponential_multiply_fusion) | copy-start | bytes 12292
  680.3 23.7 %copy-start.27 = (f32[2,4,128,64]{2,3,1,0:T(8,128)}, f32[2,4,128,64]{2,3,1,0:T(8,128)S(1)}, u32[]{:S(2)}) copy-start(f32[2,4,128,64]{2,3,1,0:T(8,128)S(1)} %get-tuple-element.233) | copy-start | bytes 786436
  681.3 336.1 %reduce-scatter.10.cloned.1.call-start = ((), (), s32[]{:S(2)}) async-start(), calls=%async_computation.10 | async-start | bytes 7077888 | tf_op jit(solution)/shard_map/reduce_scatter | solution.py:213
  731.4 222.5 %copy-start.31 = (bf16[1024,256]{1,0:T(8,128)(2,1)S(1)}, bf16[1024,256]{1,0:T(8,128)(2,1)}, u32[]{:S(2)}) copy-start(bf16[1024,256]{1,0:T(8,128)(2,1)} %param.37) | copy-start | bytes 1572868
  957.5 94.8 %all-gather.13.cloned.1.call-start = ((), (), s32[]{:S(2)}) async-start(), calls=%async_computation.11 | async-start | bytes 3538944 | tf_op jit(solution)/shard_map/all_gather | solution.py:219
  1019.4 40.1 %copy-start.67 = (bf16[1024,512]{1,0:T(8,128)(2,1)S(1)}, bf16[1024,512]{1,0:T(8,128)(2,1)}, u32[]{:S(2)}) copy-start(bf16[1024,512]{1,0:T(8,128)(2,1)} %param.35) | copy-start | bytes 3145732
  1019.4 106.5 %reduce-scatter.12.cloned.1.call-start = ((), (), s32[]{:S(2)}) async-start(), calls=%async_computation.12 | async-start | bytes 7077888 | tf_op jit(solution)/shard_map/reduce_scatter | solution.py:224
  1063.9 66.8 %copy-start.9 = (f32[2,96,1024]{2,1,0:T(8,128)S(1)}, f32[2,96,1024]{2,1,0:T(8,128)}, u32[]{:S(2)}) copy-start(f32[2,96,1024]{2,1,0:T(8,128)} %reduce-scatter.10.cloned.1.call-done) | copy-start | bytes 2359300
  1064.0 100.1 %all-gather.15.cloned.1.call-start = ((), (), s32[]{:S(2)}) async-start(), calls=%async_computation.13 | async-start | bytes 3538944 | tf_op jit(solution)/shard_map/all_gather | solution.py:234
  1131.6 168.0 %all-gather.17.cloned.1.call-start = ((), (), s32[]{:S(2)}) async-start(), calls=%async_computation.14 | async-start | bytes 9175040 | tf_op jit(solution)/shard_map/all_gather | solution.py:34
  1167.0 707.9 %reduce-scatter.14.cloned.1.call-start = ((), (), s32[]{:S(2)}) async-start(), calls=%async_computation.15 | async-start | bytes 18350080 | tf_op jit(solution)/shard_map/reduce_scatter | solution.py:242
  1630.8 244.1 %copy-start.33 = (bf16[1024,128]{1,0:T(8,128)(2,1)S(1)}, bf16[1024,128]{1,0:T(8,128)(2,1)}, u32[]{:S(2)}) copy-start(bf16[1024,128]{1,0:T(8,128)(2,1)} %param.31) | copy-start | bytes 786436
  1630.9 244.1 %copy-start.35 = (bf16[1024,128]{1,0:T(8,128)(2,1)S(1)}, bf16[1024,128]{1,0:T(8,128)(2,1)}, u32[]{:S(2)}) copy-start(bf16[1024,128]{1,0:T(8,128)(2,1)} %param.30) | copy-start | bytes 786436
  1630.9 248.2 %copy-start.23 = (bf16[2,768,128]{1,2,0:T(8,128)(2,1)S(1)}, bf16[2,768,128]{1,2,0:T(8,128)(2,1)}, u32[]{:S(2)}) copy-start(bf16[2,768,128]{1,2,0:T(8,128)(2,1)} %get-tuple-element.89) | copy-start | bytes 1179652
  1630.9 248.2 %copy-start.37 = (bf16[1024,128]{1,0:T(8,128)(2,1)S(1)}, bf16[1024,128]{1,0:T(8,128)(2,1)}, u32[]{:S(2)}) copy-start(bf16[1024,128]{1,0:T(8,128)(2,1)} %param.29) | copy-start | bytes 786436
  1630.9 343.9 %reduce-scatter.18.cloned.1.call-start = ((), (), s32[]{:S(2)}) async-start(), calls=%async_computation.17 | async-start | bytes 7077888 | tf_op jit(solution)/shard_map/reduce_scatter | solution.py:261
  1889.1 138.5 %reduce-scatter.16.cloned.1.call-start = ((), (), s32[]{:S(2)}) async-start(), calls=%async_computation.16 | async-start | bytes 9437184 | tf_op jit(solution)/shard_map/reduce_scatter | solution.py:260
  1899.6 390.8 %all-reduce.26.cloned.1.call-start = ((), (), s32[]{:S(2)}) async-start(), calls=%async_computation.19 | async-start | bytes 14680064 | tf_op jit(solution)/shard_map/psum | solution.py:282
  1921.1 14.7 copy-start.25
  1921.1 15.0 copy-start.38
  1921.1 15.3 copy-start.46
  1921.1 15.3 copy-start.47
  1921.2 40.8 %copy-start.58 = (f32[256]{0:T(256)S(1)}, f32[256]{0:T(256)}, u32[]{:S(2)}) copy-start(f32[256]{0:T(256)} %get-tuple-element.203) | copy-start | bytes 3076
  1921.2 53.6 %copy-start.40 = (f32[1024]{0:T(1024)S(1)}, f32[1024]{0:T(1024)}, u32[]{:S(2)}) copy-start(f32[1024]{0:T(1024)} %param.27) | copy-start | bytes 12292
  1929.7 48.5 %copy-start.10 = (f32[2,96,1024]{2,1,0:T(8,128)S(1)}, f32[2,96,1024]{2,1,0:T(8,128)}, u32[]{:S(2)}) copy-start(f32[2,96,1024]{2,1,0:T(8,128)} %reduce-scatter.10.cloned.1.call-done) | copy-start | bytes 2359300
  1929.7 48.5 %copy-start.12 = (f32[2,96,1024]{2,1,0:T(8,128)S(1)}, f32[2,96,1024]{2,1,0:T(8,128)}, u32[]{:S(2)}) copy-start(f32[2,96,1024]{2,1,0:T(8,128)} %copy-done.11) | copy-start | bytes 2359300
  1929.7 48.5 %copy-start.52 = (f32[2,96]{1,0:T(2,128)S(1)}, f32[2,96]{1,0:T(2,128)}, u32[]{:S(2)}) copy-start(f32[2,96]{1,0:T(2,128)} %copy-done.51) | copy-start | bytes 2308
  (51 other events, 360.8 us)
Sparse Core Ops, SparseCore 0:
  31.5 135.1 all-gather.6
  292.0 102.3 all-reduce.19
  417.7 104.2 all-reduce.21
  531.5 63.5 all-gather.8
  608.8 55.1 all-reduce.23
  681.4 22.5 all-gather.10
  957.7 59.6 reduce-scatter.9
  1020.0 32.2 all-gather.12
  1064.1 61.7 reduce-scatter.11
  1131.7 32.2 all-gather.14
  1167.1 132.4 all-gather.16
  1631.0 243.8 reduce-scatter.13
  1889.2 63.3 reduce-scatter.17
  1956.3 71.2 reduce-scatter.15
  2031.6 258.8 all-reduce.25
where the time goes:
time: 2320 us; the launch traced here: 2310 us
  waiting for transfers between devices  1330 us (57%)
  other arithmetic  300 us (13%)
  matrix products  299 us (13%)
  blocking collectives  256 us (11%)
  local copies, waits for them, and re-layouts  105 us (5%)
    all_gather x2, waiting for transfers between devices, collect_keys(): return lax.all_gather(key_value, 'seq', axis=1, tiled=True)  265 us
    psum x1, waiting for transfers between devices, on_device(): lax.psum((query_part, kv_part[:, :key_cols], kv_part[:, key_cols:], out_p...  256 us
    reduce_scatter x1, waiting for transfers between devices, on_device(): lax.psum_scatter(grad_kv, 'seq', scatter_dimension=1, tiled=True)  244 us
    unnamed x2, blocking collectives  243 us
    sub x2, other arithmetic, score_grads(): grad_shares - inner_sum[..., None]  140 us
    psum x1, waiting for transfers between devices, on_device(): lax.psum(jnp.einsum('nrf,fd->nrd', active, w_down, preferred_element_type...  104 us
    psum x1, waiting for transfers between devices, on_device(): lax.psum(jnp.einsum('nqe,ed->nqd', mixed_low, w_out, preferred_element_ty...  91.9 us
    all_gather x1, waiting for transfers between devices, on_device(): portion = lax.all_gather(tile_block, 'seq', axis=0, tiled=True)  62.8 us
  transfers between devices with their start and end apart: 15, of which 14 were waited for; matrix products, arithmetic and copies ran while one was open for 3% of the time, Pallas kernels for 0%

commit v1 on v0

v1 whole, which is shorter than its diff:
```python
import jax
import jax.numpy as jnp
from jax import lax
from jax.sharding import PartitionSpec as P

HEAD_DIM = 64
CH = 32
TRI_SIDE = 32
BF = jnp.bfloat16
F32 = jnp.float32
HIGH = lax.Precision.HIGHEST


def dot(spec, *operands):
    return jnp.einsum(spec, *operands, preferred_element_type=F32)


def standard_rows(token_rows):
    centre = jnp.mean(token_rows, axis=-1, keepdims=True)
    offset = token_rows - centre
    spread = jnp.mean(offset * offset, axis=-1, keepdims=True)
    scale = lax.rsqrt(spread + 1e-05)
    return offset * scale, scale


def norm_rows(token_rows, norm_gain, norm_shift):
    return standard_rows(token_rows)[0] * norm_gain + norm_shift


def norm_back(standard, scale, norm_gain, grad):
    scaled = grad * norm_gain
    first = jnp.mean(scaled, axis=-1, keepdims=True)
    second = jnp.mean(scaled * standard, axis=-1, keepdims=True)
    return scale * (scaled - first - standard * second)


def xor_pairs(size, mask):
    return [(i, i ^ mask) for i in range(size)]


def hyper_sum(value, axes):
    for axis in axes:
        size = lax.axis_size(axis)
        mask = 1
        while mask < size:
            value = value + lax.ppermute(value, axis, xor_pairs(size, mask))
            mask *= 2
    return value


def render(features, dec_first, dec_bias, dec_second, live_rays):
    preact = jnp.einsum("ch,...cs->...hs", dec_first, features, precision=HIGH) + dec_bias[:, None]
    hidden = jax.nn.silu(preact)
    output = jnp.einsum("hk,...hs->...ks", dec_second, hidden, precision=HIGH)
    samples = output.shape[-1]
    density = jax.nn.softplus(output[..., 0, :])
    colour = jax.nn.sigmoid(output[..., 1:, :])
    optical = density * (2.0 / samples)
    place = jnp.arange(samples)
    before = (place[:, None] < place[None, :]).astype(F32)
    through = jnp.exp(-jnp.einsum("...t,ts->...s", optical, before, precision=HIGH))
    weight = through * (1.0 - jnp.exp(-optical))
    return jnp.sum(weight[..., None, :] * colour, axis=-1) * live_rays[..., None]


def on_device(
    patch_tokens,
    plane_tokens,
    norm1_gain,
    norm1_bias,
    w_query,
    w_key,
    w_value,
    w_out,
    norm2_gain,
    norm2_bias,
    w_up,
    w_down,
    w_unpatch,
    b_unpatch,
    w_dec1,
    b_dec1,
    w_dec2,
    tile_index,
    corner_weights,
    ray_count,
    color_grad,
):
    scenes, patch_local, width = patch_tokens.shape
    plane_local = plane_tokens.shape[1]
    seq_count, tp_count = lax.axis_size("seq"), lax.axis_size("tp")
    seq_rank, tp_rank = lax.axis_index("seq"), lax.axis_index("tp")
    own_patch = patch_local // tp_count
    own_plane = plane_local // tp_count
    cols = w_query.shape[1]
    heads = cols // HEAD_DIM
    ray_seq = tile_index.shape[2]
    rays = ray_seq // tp_count
    picks = 3 * rays
    seq_picks = tp_count * scenes * picks
    all_picks = seq_count * seq_picks
    score_scale = HEAD_DIM**-0.5

    base = (jnp.arange(3, dtype=jnp.int32) * (TRI_SIDE * TRI_SIDE))[None, :, None]
    ids = (tile_index + base).reshape(scenes, 3, tp_count, rays)
    ids = jnp.transpose(ids, (2, 0, 1, 3)).reshape(tp_count, scenes, picks)
    ids = lax.all_gather(ids, "seq", axis=0)
    local_ids = ids - seq_rank * plane_local
    inside = (local_ids >= 0) & (local_ids < plane_local)
    scene_base = (jnp.arange(scenes, dtype=jnp.int32) * plane_local)[None, None, :, None]
    row_ids = jnp.where(inside, local_ids + scene_base, -1).reshape(all_picks)
    onehot = (
        row_ids[:, None] == jnp.arange(scenes * plane_local, dtype=jnp.int32)[None, :]
    ).astype(BF)

    w_out_all = lax.all_gather(w_out, "tp", axis=0)
    bias_high = b_unpatch.astype(BF)
    rest = b_unpatch - bias_high.astype(F32)
    bias_mid = rest.astype(BF)
    bias_low = (rest - bias_mid.astype(F32)).astype(BF)
    bias_rows = jnp.stack([bias_high, bias_mid, bias_low] + [jnp.zeros_like(bias_high)] * 13)
    unpatch_all = lax.all_gather(jnp.concatenate([w_unpatch, bias_rows]), "tp", axis=0)
    qkv_weight = jnp.concatenate([w_key, w_value, w_query], axis=1)
    qkv_all = lax.all_gather(qkv_weight, "tp", axis=0)
    key_weight = qkv_weight[:, : 2 * cols]

    corners = corner_weights.reshape(
        scenes, tp_count, rays, 3, corner_weights.shape[3], corner_weights.shape[4]
    )
    corners = lax.all_to_all(jnp.moveaxis(corners, 1, 0), "tp", 0, 0, tiled=True)

    picked_rows = lax.psum_scatter(
        jnp.dot(onehot, plane_tokens.reshape(-1, width)), "seq", scatter_dimension=0, tiled=True
    )

    plane_normed = norm_rows(plane_tokens.astype(F32), norm1_gain, norm1_bias).astype(BF)
    patch_normed = norm_rows(patch_tokens.astype(F32), norm1_gain, norm1_bias).astype(BF)
    query_rows = dot("nrd,de->nre", plane_normed, w_query).astype(BF)
    queries = hyper_sum(jnp.dot(onehot, query_rows.reshape(-1, cols)), ("seq",))
    normed = jnp.concatenate([patch_normed, plane_normed], axis=1)
    key_value = dot("nrd,de->nre", normed, key_weight).astype(BF)

    def by_scene(value):
        value = value.reshape(seq_count, tp_count, scenes, picks, -1)
        return jnp.moveaxis(value, 2, 0).reshape(scenes, seq_count * tp_count * picks, -1)

    def by_seq(value):
        value = value.reshape(scenes, seq_count, tp_count, picks, -1)
        return jnp.moveaxis(value, 0, 2).reshape(seq_count, seq_picks, -1)

    def in_heads(value):
        return value.reshape(value.shape[:-1] + (heads, HEAD_DIM))

    query_heads = in_heads(by_scene(queries))
    key_heads = in_heads(key_value[..., :cols])
    value_heads = in_heads(key_value[..., cols:])
    scores = dot("nqhd,nkhd->nhqk", query_heads, key_heads) * score_scale
    row_max = jnp.max(scores, axis=-1, keepdims=True)
    raised = jnp.exp(scores - row_max)
    row_total = jnp.sum(raised, axis=-1)
    part = dot("nhqk,nkhd->nqhd", raised.astype(BF), value_heads)
    part = part / jnp.moveaxis(row_total, 1, 2)[..., None]
    logsum = row_max[..., 0] + jnp.log(row_total)
    part = by_seq(part.astype(BF).reshape(scenes, -1, cols))
    part = lax.all_to_all(part, "seq", 0, 0, tiled=True)
    logsum_parts = lax.all_gather(logsum, "seq", axis=0)
    top = jnp.max(logsum_parts, axis=0)
    logsum = top + jnp.log(jnp.sum(jnp.exp(logsum_parts - top), axis=0))
    share = jnp.exp(logsum_parts - logsum)
    share = share.reshape(seq_count, scenes, heads, seq_count, tp_count, picks)
    share = lax.dynamic_index_in_dim(share, seq_rank, 3, keepdims=False)
    share = jnp.transpose(share, (0, 3, 1, 4, 2)).reshape(seq_count, seq_picks, heads, 1)
    mixed = jnp.sum(in_heads(part.astype(F32)) * share, axis=0).reshape(seq_picks, cols)
    mixed_low = mixed.astype(BF)

    mixed_all = lax.all_gather(mixed_low, "tp", axis=0)
    branch = dot("tre,ted->rd", mixed_all, w_out_all)
    hidden_state = picked_rows.astype(F32) + branch
    normed2 = norm_rows(hidden_state, norm2_gain, norm2_bias).astype(BF)
    preact = jnp.dot(normed2, w_up, preferred_element_type=F32)
    active = jax.nn.gelu(preact).astype(BF)
    down = jnp.dot(active, w_down, preferred_element_type=F32).astype(BF)
    own_rows = scenes * picks

    def sum_own(value):
        value = lax.all_to_all(value.reshape(tp_count, own_rows, width), "tp", 0, 0, tiled=True)
        return jnp.sum(value.astype(F32), axis=0)

    hidden_own = lax.dynamic_slice_in_dim(hidden_state, tp_rank * own_rows, own_rows, 0)
    result_own = (hidden_own + sum_own(down)).astype(BF)
    ones = jnp.ones((own_rows, 3), BF)
    result_wide = jnp.concatenate([result_own, ones, jnp.zeros((own_rows, 13), BF)], axis=1)
    tiles = dot("kd,tdc->ktc", result_wide, unpatch_all).astype(BF)
    tile_cols = tiles.shape[2]
    pixels = tile_cols // CH
    picked = tiles.reshape(scenes, 3, rays, tp_count, pixels, CH)
    features = dot("nprtxc,tnrpxs->nrcs", picked, corners)
    first_ray = (seq_rank * tp_count + tp_rank) * rays
    live_rays = (
        (first_ray + jnp.arange(rays, dtype=jnp.int32))[None, :] < ray_count[:, None]
    ).astype(F32)

    def draw_colours(feature_rows, dec_first, dec_bias, dec_second):
        return render(feature_rows, dec_first, dec_bias, dec_second, live_rays)

    colours, pullback = jax.vjp(draw_colours, features, w_dec1, b_dec1, w_dec2)
    grad_features, dec1_part, dec1_bias_part, dec2_part = pullback(jnp.moveaxis(color_grad, 1, -1))
    grad_tiles = jnp.einsum(
        "nrcs,tnrpxs->nprtxc", grad_features, corners.astype(F32), precision=HIGH
    ).astype(BF)
    grad_tiles = grad_tiles.reshape(own_rows, tp_count, tile_cols)
    unpatch_bias_part = jnp.sum(grad_tiles.astype(F32), axis=0).reshape(-1)
    grad_result = dot("ktc,tdc->kd", grad_tiles, unpatch_all[:, :width])
    grad_tile_cols = lax.all_to_all(jnp.moveaxis(grad_tiles, 1, 0), "tp", 0, 0, tiled=True)
    result_all = lax.all_gather(result_own, "tp", axis=0, tiled=True)
    unpatch_part = dot("rd,rc->dc", result_all, grad_tile_cols.reshape(seq_picks, tile_cols))

    result_rows = lax.all_gather(grad_result.astype(BF), "tp", axis=0, tiled=True)
    down_part = dot("rf,rd->fd", active, result_rows)
    grad_active = dot("rd,fd->rf", result_rows, w_down)
    grad_preact = jax.vjp(jax.nn.gelu, preact)[1](grad_active)[0].astype(BF)
    up_part = dot("rd,rf->df", normed2, grad_preact)
    grad_normed2 = sum_own(dot("rf,df->rd", grad_preact, w_up).astype(BF))
    standard2, scale2 = standard_rows(hidden_own)
    gain2_part = jnp.sum(grad_normed2 * standard2, axis=0)
    shift2_part = jnp.sum(grad_normed2, axis=0)
    grad_hidden = grad_result + norm_back(standard2, scale2, norm2_gain, grad_normed2)
    hidden_rows = lax.all_gather(grad_hidden.astype(BF), "tp", axis=0, tiled=True)
    out_part = dot("re,rd->ed", mixed_low, hidden_rows)
    grad_mixed = dot("rd,ed->re", hidden_rows, w_out).astype(BF)
    inner = jnp.sum(in_heads(mixed * grad_mixed.astype(F32)), axis=-1)
    inner = lax.all_gather(inner.T, "seq", axis=0)
    inner = inner.reshape(seq_count, heads, tp_count, scenes, picks)
    inner = jnp.transpose(inner, (3, 1, 0, 2, 4)).reshape(scenes, heads, -1)
    hidden_cols = lax.dynamic_slice_in_dim(hidden_rows, tp_rank * cols, cols, 1)
    sent = lax.all_gather(jnp.concatenate([grad_mixed, hidden_cols], axis=1), "seq", axis=0)
    grad_heads = in_heads(by_scene(sent[..., :cols]))
    hidden_cols = sent[..., cols:].reshape(all_picks, cols)

    scores = dot("nqhd,nkhd->nhqk", query_heads, key_heads) * score_scale
    shares = jnp.exp(scores - logsum[..., None])
    grad_shares = dot("nqhd,nkhd->nhqk", grad_heads, value_heads)
    grad_scores = (shares * (grad_shares - inner[..., None])).astype(BF) * BF(score_scale)
    grad_query = dot("nhqk,nkhd->nqhd", grad_scores, key_heads)
    grad_key = dot("nhqk,nqhd->nkhd", grad_scores, query_heads)
    grad_value = dot("nhqk,nqhd->nkhd", shares.astype(BF), grad_heads)

    def flat(value):
        return value.reshape(value.shape[:2] + (cols,))

    grad_kv = jnp.concatenate([flat(grad_key), flat(grad_value)], axis=-1).astype(BF)
    grad_query = by_seq(flat(grad_query).astype(BF)).reshape(all_picks, cols)
    grad_query = hyper_sum(grad_query, ("seq",))
    scattered = dot("kr,kd->rd", onehot, jnp.concatenate([grad_query, hidden_cols], axis=1))
    scattered = scattered.astype(BF).reshape(scenes, plane_local, 2 * cols)
    grad_query = scattered[..., :cols]
    query_part = dot("nrd,nre->de", plane_normed, grad_query)
    kv_part = dot("nrd,nre->de", normed, grad_kv)

    kv_sum = jnp.sum(grad_kv.astype(F32), axis=(0, 1))
    query_sum = jnp.sum(grad_query.astype(F32), axis=(0, 1))
    key_wide, query_wide = key_weight.astype(F32), w_query.astype(F32)
    shift1_part = jnp.sum(key_wide * kv_sum, axis=1) + jnp.sum(query_wide * query_sum, axis=1)
    product = jnp.sum(key_wide * kv_part, axis=1) + jnp.sum(query_wide * query_part, axis=1)
    gain1_part = (product - norm1_bias * shift1_part) / norm1_gain

    small = [gain1_part, shift1_part, gain2_part, shift2_part, unpatch_bias_part]
    small += [dec1_part.reshape(-1), dec1_bias_part, dec2_part.reshape(-1)]
    ends = [0]
    for piece in small:
        ends.append(ends[-1] + piece.shape[0])
    small = hyper_sum(jnp.concatenate(small), ("tp", "seq"))
    small = [small[a:b] for a, b in zip(ends, ends[1:])]

    def own_piece(value, axis=0):
        size = value.shape[axis] // tp_count
        return lax.dynamic_slice_in_dim(value, tp_rank * size, size, axis)

    dec1_grad = own_piece(small[5].reshape(w_dec1.shape), 1)
    dec2_grad = own_piece(small[7].reshape(w_dec2.shape), 0)

    patch_sent = grad_kv[:, :patch_local].reshape(scenes, tp_count, own_patch, 2 * cols)
    patch_sent = lax.all_to_all(jnp.moveaxis(patch_sent, 1, 0), "tp", 0, 0, tiled=True)
    plane_sent = jnp.concatenate([grad_kv[:, patch_local:], scattered], axis=-1)
    plane_sent = plane_sent.reshape(scenes, tp_count, own_plane, 4 * cols)
    plane_sent = lax.all_to_all(jnp.moveaxis(plane_sent, 1, 0), "tp", 0, 0, tiled=True)
    patch_part = dot("tnre,tde->nrd", patch_sent, qkv_all[..., : 2 * cols])
    plane_part = dot("tnre,tde->nrd", plane_sent[..., : 3 * cols], qkv_all)
    plane_extra = jnp.moveaxis(plane_sent[..., 3 * cols :], 0, 2).reshape(scenes, own_plane, width)

    def own_grad(token_rows, own, grad):
        rows = lax.dynamic_slice_in_dim(token_rows, tp_rank * own, own, 1).astype(F32)
        standard, scale = standard_rows(rows)
        return norm_back(standard, scale, norm1_gain, grad)

    patch_grad = own_grad(patch_tokens, own_patch, patch_part)
    plane_grad = own_grad(plane_tokens, own_plane, plane_part) + plane_extra.astype(F32)

    first = (out_part, up_part, down_part, unpatch_part)
    first = lax.psum(tuple(value.astype(BF) for value in first), "seq")
    second = lax.psum((query_part.astype(BF), kv_part.astype(BF)), "seq")
    first = [value.astype(F32) for value in first]
    second = [value.astype(F32) for value in second]
    return (
        jnp.moveaxis(colours, -1, 1),
        patch_grad,
        plane_grad,
        own_piece(small[0]),
        own_piece(small[1]),
        second[0],
        second[1][:, :cols],
        second[1][:, cols:],
        first[0],
        own_piece(small[2]),
        own_piece(small[3]),
        first[1],
        first[2],
        first[3],
        own_piece(small[4]),
        dec1_grad,
        own_piece(small[6]),
        dec2_grad,
    )


def solution(mesh):
    in_specs = (
        P(None, "seq", None),
        P(None, "seq", None),
        P(),
        P(),
        P(None, "tp"),
        P(None, "tp"),
        P(None, "tp"),
        P("tp", None),
        P(),
        P(),
        P(None, "tp"),
        P("tp", None),
        P(None, "tp"),
        P("tp"),
        P(),
        P(),
        P(),
        P(None, None, "seq"),
        P(None, "seq", None, "tp", None),
        P(),
        P(None, None, ("seq", "tp")),
    )
    out_specs = (
        P(None, None, ("seq", "tp")),
        P(None, ("seq", "tp"), None),
        P(None, ("seq", "tp"), None),
        P("tp"),
        P("tp"),
        P(None, "tp"),
        P(None, "tp"),
        P(None, "tp"),
        P("tp", None),
        P("tp"),
        P("tp"),
        P(None, "tp"),
        P("tp", None),
        P(None, "tp"),
        P("tp"),
        P(None, "tp"),
        P("tp"),
        P("tp", None),
    )
    return jax.shard_map(
        on_device, mesh=mesh, in_specs=in_specs, out_specs=out_specs, check_vma=False
    )
```

time: 2320 us -> 475 us (0.20)
  waiting for transfers between devices: 1330 us -> 151 us
  other arithmetic: 300 us -> 42.5 us
  matrix products: 299 us -> 82.3 us
  blocking collectives: 256 us -> 95.2 us
  local copies, waits for them, and re-layouts: 105 us -> 44.7 us
  starting transfers between devices: 1.55 us -> 36.9 us
    all_gather x6 -> x3, waiting for transfers between devices: 414 us -> 0.03 us  [the longest x1 0.03 us: on_device(): qkv_all = lax.all_gather(qkv_weight, 'tp', axis=0)]
    reduce_scatter x5 -> x1, waiting for transfers between devices: 410 us -> 0.01 us  [on_device(): lax.psum_scatter(jnp.dot(onehot, plane_tokens.reshape(-1, width)), 'seq',...]
    psum x3 -> x1, waiting for transfers between devices: 452 us -> 73.6 us  [on_device(): second = lax.psum((query_part.astype(BF), kv_part.astype(BF)), 'seq')]
    unnamed x2 -> x0, blocking collectives: 243 us -> none
    dot_general x40 -> x37, matrix products: 299 us -> 82.3 us  [the longest x24 64.4 us: dot(): return jnp.einsum(spec, *operands, preferred_element_type=F32)]
    sub x2 -> x0, other arithmetic: 140 us -> none  [score_grads(): grad_shares - inner_sum[..., None]]
    all_gather x0 -> x8, blocking collectives: none -> 95.2 us  [the longest x1 14.8 us: on_device(): ids = lax.all_gather(ids, 'seq', axis=0)]
    reduce_sum x19 -> x21, other arithmetic: 82.3 us -> 18.5 us  [the longest x5 7.94 us: standard_rows(): centre = jnp.mean(token_rows, axis=-1, keepdims=True)]
  transfers between devices with their start and end apart: 15 -> 21, of which waited for: 14 -> 11; matrix products, arithmetic and copies ran while one was open for 3% -> 30% of each run, Pallas kernels for 0% -> 0%
where the time goes in v1:
time: 475 us; the launch traced here: 470 us
  waiting for transfers between devices  151 us (32%)
  blocking collectives  95.2 us (20%)
  matrix products  82.3 us (17%)
  local copies, waits for them, and re-layouts  44.7 us (9%)
  other arithmetic  42.5 us (9%)
  starting transfers between devices  36.9 us (8%)
  between operations  17.3 us (4%)
    psum x1, waiting for transfers between devices, on_device(): second = lax.psum((query_part.astype(BF), kv_part.astype(BF)), 'seq')  73.6 us
    dot_general x24, matrix products, dot(): return jnp.einsum(spec, *operands, preferred_element_type=F32)  64.4 us
    ppermute x9, waiting for transfers between devices, hyper_sum(): value = value + lax.ppermute(value, axis, xor_pairs(size, mask))  47 us
    unnamed x153, local copies, waits for them, and re-layouts  17.6 us
    all_gather x1, blocking collectives, on_device(): ids = lax.all_gather(ids, 'seq', axis=0)  14.8 us
    all_gather x1, blocking collectives, on_device(): lax.all_gather(jnp.concatenate([grad_mixed, hidden_cols], axis=1), 'seq',...  14.7 us
    all_to_all x2, waiting for transfers between devices, sum_own(): lax.all_to_all(value.reshape(tp_count, own_rows, width), 'tp', 0, 0, tile...  14.6 us
    all_gather x1, blocking collectives, on_device(): logsum_parts = lax.all_gather(logsum, 'seq', axis=0)  13.6 us
  transfers between devices with their start and end apart: 21, of which 11 were waited for; matrix products, arithmetic and copies ran while one was open for 30% of the time, Pallas kernels for 0%

profile of v1, /device:TPU:0, one launch (start us, length us, event | category | flops | bytes accessed | tf_op | source)
XLA Modules:
  0.0 470.2 jit_solution(13249796717671157547)
XLA Ops:
  9.2 14.8 %all_gather.50 = s32[4,8,2,12]{3,1,2,0:T(8,128)S(1)} all-gather(s32[1,8,2,12]{3,1,2,0:T(8,128)S(1)} %copy.302), channel_id=1, replica_groups=mesh['seq'=4,'tp'=8] {'seq'}, dimensions={0}, use_global_device_ids=true | all-gather | bytes 3840 | tf_op jit(solution)/shard_map/all_gather | solution.py:107
  24.3 5.8 %fusion.29 = bf16[768,1024]{1,0:T(8,128)(2,1)} fusion(bf16[1536,1024]{1,0:T(8,128)(2,1)} %bitcast.252, s32[768]{0:T(1024)S(1)} %eq.23), kind=kOutput, calls=%fused_computation.37 | convolution fusion | flops 2417098752 | bytes 4721664 | tf_op jit(solution)/shard_map/dot_general | solution.py:133
  30.8 2.6 concatenate.47
  33.5 2.5 convert_reduce_fusion.1
  46.4 3.0 convert_reduce_fusion
  53.5 2.4 fusion.33
  62.2 2.5 collective-permute-start.1
  64.7 11.6 %collective-permute-done.1 = bf16[768,128]{1,0:T(8,128)(2,1)S(1)} collective-permute-done((bf16[768,128]{1,0:T(8,128)(2,1)S(1)}, bf16[768,128]{1,0:T(8,128)(2,1)S(1)}, u32[]{:S(2)}, u32[]{:S(2)}) %collective-permute-start.1) | collective-permute-done | bytes 196640 | tf_op jit(solution)/shard_map/ppermute | solution.py:46
  77.4 2.9 multiply_reduce_fusion
  84.5 13.6 %all-gather = f32[8,2,384]{2,1,0:T(2,128)S(1)} all-gather(f32[2,2,384]{2,1,0:T(2,128)S(1)} %log_add_fusion.1), channel_id=2, replica_groups=mesh['seq'=4,'tp'=8] {'seq'}, dimensions={0}, use_global_device_ids=true | all-gather | bytes 30720 | tf_op jit(solution)/shard_map/all_gather | solution.py:166
  98.2 6.3 %fusion.82 = bf16[2,384,2,64]{1,3,2,0:T(8,128)(2,1)S(1)} fusion(bf16[2,1792,2,64]{1,3,2,0:T(8,128)(2,1)S(1)} %bitcast.263, f32[2,2,384,1792]{3,2,1,0:T(8,128)} %copy-done.2, f32[2,2,384]{2,1,0:T(2,128)S(1)} %get-tuple-element.206, f32[2,384,2]{1,2,0:T(2,128)S(1)} %bitcast.292), kind=kOutput, calls=%fused_computation.108 | convolution fusion | flops 360775680 | bytes 12136448 | tf_op jit(solution)/shard_map/nhqk,nkhd->nqhd/dot_general | solution.py:15
  106.2 3.4 all-to-all-start
  110.1 5.7 %all-to-all-done = bf16[4,192,128]{2,1,0:T(8,128)(2,1)S(1)} async-done(((bf16[4,192,128]{2,1,0:T(8,128)(2,1)}), bf16[4,192,128]{2,1,0:T(8,128)(2,1)S(1)}, u32[]{:S(2)}, u32[]{:S(2)}) %all-to-all-start) | async-done | bytes 196640 | tf_op jit(solution)/shard_map/all_to_all | solution.py:165
  116.7 9.9 %all-gather.1 = bf16[1536,128]{1,0:T(8,128)(2,1)S(1)} all-gather(bf16[192,128]{1,0:T(8,128)(2,1)S(1)} %copy.313), channel_id=3, replica_groups=mesh['seq'=4,'tp'=8] {'tp'}, dimensions={0}, use_global_device_ids=true | all-gather | bytes 442368 | tf_op jit(solution)/shard_map/all_gather | solution.py:176
  132.0 3.5 all-to-all-start.1
  138.3 10.0 %all-to-all-done.1 = bf16[8,24,1024]{2,1,0:T(8,128)(2,1)S(1)} async-done(((bf16[8,24,1024]{2,1,0:T(8,128)(2,1)}), bf16[8,24,1024]{2,1,0:T(8,128)(2,1)S(1)}, u32[]{:S(2)}, u32[]{:S(2)}) %all-to-all-start.1) | async-done | bytes 393248 | tf_op jit(solution)/shard_map/all_to_all | solution.py:186
  148.3 4.1 all-to-all-start.2
  153.2 11.5 %all_gather.65 = bf16[192,1024]{1,0:T(8,128)(2,1)S(1)} all-gather(bf16[24,1024]{1,0:T(8,128)(2,1)S(1)} %get-tuple-element.191), channel_id=1, replica_groups=mesh['seq'=4,'tp'=8] {'tp'}, dimensions={0}, use_global_device_ids=true | all-gather | bytes 442368 | tf_op jit(solution)/shard_map/all_gather | solution.py:215
  164.8 2.9 convolution_convert_fusion.8
  182.1 4.0 all-to-all-start.6
  188.9 4.2 fusion.178
  193.1 10.1 %all_gather.57 = bf16[192,1024]{1,0:T(8,128)(2,1)S(1)} all-gather(bf16[24,1024]{1,0:T(8,128)(2,1)S(1)} %get-tuple-element.214), channel_id=1, replica_groups=mesh['seq'=4,'tp'=8] {'tp'}, dimensions={0}, use_global_device_ids=true | all-gather | bytes 442368 | tf_op jit(solution)/shard_map/all_gather | solution.py:218
  208.7 3.5 all-to-all-start.3
  215.9 4.5 all-to-all-done.3
  221.8 8.6 %all_gather.58 = bf16[192,1024]{1,0:T(8,128)(2,1)S(1)} all-gather(bf16[24,1024]{1,0:T(8,128)(2,1)S(1)} %add_convert_fusion.1), channel_id=1, replica_groups=mesh['seq'=4,'tp'=8] {'tp'}, dimensions={0}, use_global_device_ids=true | all-gather | bytes 442368 | tf_op jit(solution)/shard_map/all_gather | solution.py:228
  230.7 14.7 %all-gather.4 = bf16[768,256]{1,0:T(8,128)(2,1)S(1)} all-gather(bf16[192,256]{1,0:T(8,128)(2,1)S(1)} %pad_maximum_fusion.12), channel_id=6, replica_groups=mesh['seq'=4,'tp'=8] {'seq'}, dimensions={0}, use_global_device_ids=true | all-gather | bytes 491520 | tf_op jit(solution)/shard_map/all_gather | solution.py:236
  247.5 12.0 %all-gather.7 = f32[4,2,192]{2,1,0:T(2,128)S(1)} all-gather(f32[1,2,192]{2,1,0:T(2,128)S(1)} %bitcast.294), channel_id=7, replica_groups=mesh['seq'=4,'tp'=8] {'seq'}, dimensions={0}, use_global_device_ids=true | all-gather | bytes 7680 | tf_op jit(solution)/shard_map/all_gather | solution.py:232
  259.8 5.8 %multiply_convert_fusion = bf16[2,2,384,1792]{3,2,1,0:T(8,128)(2,1)S(1)} fusion(f32[2,2,384,1792]{3,2,1,0:T(8,128)} %copy-done.2, bf16[2,384,2,64]{1,3,2,0:T(8,128)(2,1)S(1)} %copy.323, bf16[2,1792,2,64]{1,3,2,0:T(8,128)(2,1)S(1)} %bitcast.264, f32[2,2,384]{2,1,0:T(2,128)S(1)} %sub.192, f32[2,2,384]{2,1,0:T(2,128)S(1)} %log_add_fusion), kind=kOutput, calls=%fused_computation | convolution fusion | flops 366084096 | bytes 17641472 | tf_op jit(solution)/shard_map/nqhd,nkhd->nhqk/dot_general | solution.py:15
  265.6 2.4 copy-done.8
  272.7 6.3 %fusion.40 = bf16[2,2,64,1792]{3,2,1,0:T(8,128)(2,1)S(1)} fusion(bf16[2,384,2,64]{1,3,2,0:T(8,128)(2,1)S(1)} %copy.323, f32[2,2,384,1792]{3,2,1,0:T(8,128)} %copy-done.2, f32[2,2,384]{2,1,0:T(2,128)S(1)} %log_add_fusion), kind=kOutput, calls=%fused_computation.48 | convolution fusion | flops 361037824 | bytes 12130304 | tf_op jit(solution)/shard_map/nhqk,nqhd->nkhd/dot_general | solution.py:15
  283.4 3.0 fusion.76
  287.6 3.4 collective-permute-done.3
  291.0 2.5 fusion.36
  295.6 3.2 fusion.95
  301.6 4.4 all-to-all-start.5
  309.2 17.6 %collective-permute-done.5 = f32[8512]{0:T(1024)S(1)} collective-permute-done((f32[8512]{0:T(1024)S(1)}, f32[8512]{0:T(1024)S(1)}, u32[]{:S(2)}, u32[]{:S(2)}) %collective-permute-start.5) | collective-permute-done | bytes 34080 | tf_op jit(solution)/shard_map/ppermute | solution.py:46
  328.3 2.5 collective-permute-done.6
  331.5 5.6 %collective-permute-done.7 = f32[8512]{0:T(1024)S(1)} collective-permute-done((f32[8512]{0:T(1024)S(1)}, f32[8512]{0:T(1024)S(1)}, u32[]{:S(2)}, u32[]{:S(2)}) %collective-permute-start.7) | collective-permute-done | bytes 34080 | tf_op jit(solution)/shard_map/ppermute | solution.py:46
  339.1 6.3 %collective-permute-done.8 = f32[8512]{0:T(1024)S(1)} collective-permute-done((f32[8512]{0:T(1024)S(1)}, f32[8512]{0:T(1024)S(1)}, u32[]{:S(2)}, u32[]{:S(2)}) %collective-permute-start.8) | collective-permute-done | bytes 34080 | tf_op jit(solution)/shard_map/ppermute | solution.py:46
  350.7 3.6 all-to-all-start.4
  354.3 5.5 %fusion.170 = (f32[2,96]{1,0:T(2,128)S(1)}, f32[2,96]{1,0:T(2,128)S(1)}, f32[2,96,1024]{2,1,0:T(8,128)S(1)}) fusion(f32[2,96]{1,0:T(2,128)S(1)} %copy-done.59, f32[2,96]{1,0:T(2,128)S(1)} %copy-done.52, bf16[2,768,1024]{2,1,0:T(8,128)(2,1)} %param.22, s32[]{:T(128)S(6)} %select_n.49, f32[1024]{0:T(1024)S(1)} %copy-done.42, ...), kind=kOutput, calls=%fused_computation.276 | convolution fusion | flops 1209335296 | bytes 8657924 | tf_op jit(solution)/shard_map/tnre,tde->nrd/dot_general | solution.py:15
  359.8 9.8 %all-to-all-done.4 = bf16[8,2,128,256]{3,2,1,0:T(8,128)(2,1)S(1)} async-done(((bf16[8,2,128,256]{3,2,1,0:T(8,128)(2,1)}), bf16[8,2,128,256]{3,2,1,0:T(8,128)(2,1)S(1)}, u32[]{:S(2)}, u32[]{:S(2)}) %all-to-all-start.4) | async-done | bytes 1048608 | tf_op jit(solution)/shard_map/all_to_all | solution.py:283
  369.6 3.8 fusion.169
  373.4 2.3 fusion.92
  375.7 2.4 fusion.74
  378.0 73.6 %all-reduce.5.cloned.1.call-done = (bf16[1024,128]{0,1:T(8,128)(2,1)}, bf16[1024,256]{0,1:T(8,128)(2,1)}, bf16[128,1024]{1,0:T(8,128)(2,1)}, bf16[1024,512]{1,0:...) async-done(((bf16[1024,128]{0,1:T(8,128)(2,1)}, bf16[1024,256]{0,1:T(8,128)(2,1)}, bf16[128,1024]{1,0:T(8,128)(2,1)}, bf16[1024,512]{1,0:T(8,128)(2,1)}, ...) | async-done | bytes 3670032 | tf_op jit(solution)/shard_map/psum | solution.py:301
  451.6 2.9 convert_element_type.256
  454.5 2.9 convert_element_type.258
  (349 shorter events, 102.8 us)
Async XLA Ops:
  8.0 122.8 %copy-start = (bf16[512,1024]{1,0:T(8,128)(2,1)S(1)}, bf16[512,1024]{1,0:T(8,128)(2,1)}, u32[]{:S(2)}) copy-start(bf16[512,1024]{1,0:T(8,128)(2,1)} %param.32) | copy-start | bytes 3145732
  8.0 118.5 %reduce-scatter.2.cloned.1.call-start = ((), (), s32[]{:S(2)}) async-start(), calls=%async_computation.8 | async-start | bytes 1966080 | tf_op jit(solution)/shard_map/reduce_scatter | solution.py:132
  24.2 17.4 %copy-start.61 = (s32[768]{0:T(1024)}, s32[768]{0:T(1024)S(1)}, u32[]{:S(2)}) copy-start(s32[768]{0:T(1024)S(1)} %eq.23) | copy-start | bytes 9220
  30.1 96.5 %all-gather.12.cloned.1.call-start = ((), (), s32[]{:S(2)}) async-start(), calls=%async_computation.9 | async-start | bytes 2359296 | tf_op jit(solution)/shard_map/all_gather | solution.py:116
  30.7 134.1 %all-gather.14.cloned.1.call-start = ((), (), s32[]{:S(2)}) async-start(), calls=%async_computation.10 | async-start | bytes 4792320 | tf_op jit(solution)/shard_map/all_gather | solution.py:122
  33.5 320.8 %all-gather.16.cloned.1.call-start = ((), (), s32[]{:S(2)}) async-start(), calls=%async_computation.11 | async-start | bytes 7077888 | tf_op jit(solution)/shard_map/all_gather | solution.py:124
  42.6 19.5 %collective-permute-start = (bf16[768,128]{1,0:T(8,128)(2,1)S(1)}, bf16[768,128]{1,0:T(8,128)(2,1)S(1)}, u32[]{:S(2)}, u32[]{:S(2)}) collective-permute-start(bf16[768,128]{1,0:T(8,128)(2,1)S(1)} %fusion.28), channel_id=1, source_target_pairs={{0,8},{8,0},{16,24},{24,16},{1,9},{9,1},{17,25},{25,17},{2,10},{10... | collective-permute-start | bytes 589832 | tf_op jit(solution)/shard_map/ppermute | solution.py:46
  57.8 22.5 %copy-start.55 = (f32[2,4]{1,0:T(2,128)}, f32[2,4]{1,0:T(2,128)S(1)}, u32[]{:S(2)}) copy-start(f32[2,4]{1,0:T(2,128)S(1)} %compare_convert_fusion) | copy-start | bytes 100
  59.1 21.2 %copy-start.51 = (f32[2,96]{1,0:T(2,128)}, f32[2,96]{1,0:T(2,128)S(1)}, u32[]{:S(2)}) copy-start(f32[2,96]{1,0:T(2,128)S(1)} %broadcast_multiply_fusion.4) | copy-start | bytes 2308
  62.2 14.1 %collective-permute-start.1 = (bf16[768,128]{1,0:T(8,128)(2,1)S(1)}, bf16[768,128]{1,0:T(8,128)(2,1)S(1)}, u32[]{:S(2)}, u32[]{:S(2)}) collective-permute-start(bf16[768,128]{1,0:T(8,128)(2,1)S(1)} %add.276), channel_id=1, source_target_pairs={{0,16},{8,24},{16,0},{24,8},{1,17},{9,25},{17,1},{25,9},{2,18},{10... | collective-permute-start | bytes 589832 | tf_op jit(solution)/shard_map/ppermute | solution.py:46
  64.7 70.8 %copy-start.53 = (f32[2,128]{1,0:T(2,128)}, f32[2,128]{1,0:T(2,128)S(1)}, u32[]{:S(2)}) copy-start(f32[2,128]{1,0:T(2,128)S(1)} %broadcast_multiply_fusion.7) | copy-start | bytes 3076
  105.1 24.1 %copy-start.39 = (f32[1024]{0:T(1024)S(1)}, f32[1024]{0:T(1024)}, u32[]{:S(2)}) copy-start(f32[1024]{0:T(1024)} %param.29) | copy-start | bytes 12292
  105.1 24.1 %copy-start.45 = (f32[1024]{0:T(1024)S(1)}, f32[1024]{0:T(1024)}, u32[]{:S(2)}) copy-start(f32[1024]{0:T(1024)} %param.30) | copy-start | bytes 12292
  106.2 9.6 %all-to-all-start = ((bf16[4,192,128]{2,1,0:T(8,128)(2,1)}), bf16[4,192,128]{2,1,0:T(8,128)(2,1)S(1)}, u32[]{:S(2)}, u32[]{:S(2)}) async-start(bf16[4,192,128]{2,1,0:T(8,128)(2,1)} %copy.310), calls=%async_computation.1 | async-start | bytes 393216 | tf_op jit(solution)/shard_map/all_to_all | solution.py:165
  128.9 35.8 %copy-start.43 = (f32[192]{0:T(256)}, f32[192]{0:T(256)S(1)}, u32[]{:S(2)}) copy-start(f32[192]{0:T(256)S(1)} %broadcast_multiply_fusion.8) | copy-start | bytes 2308
  129.2 35.5 %copy-start.49 = (f32[192]{0:T(256)}, f32[192]{0:T(256)S(1)}, u32[]{:S(2)}) copy-start(f32[192]{0:T(256)S(1)} %add_rsqrt_fusion.4) | copy-start | bytes 2308
  132.0 16.3 %all-to-all-start.1 = ((bf16[8,24,1024]{2,1,0:T(8,128)(2,1)}), bf16[8,24,1024]{2,1,0:T(8,128)(2,1)S(1)}, u32[]{:S(2)}, u32[]{:S(2)}) async-start(bf16[8,24,1024]{2,1,0:T(8,128)(2,1)} %bitcast.285), calls=%async_computation.2 | async-start | bytes 786432 | tf_op jit(solution)/shard_map/all_to_all | solution.py:186
  138.2 26.4 %copy-start.57 = (f32[24]{0:T(128)}, f32[24]{0:T(128)S(1)}, u32[]{:S(2)}) copy-start(f32[24]{0:T(128)S(1)} %broadcast_multiply_fusion.11) | copy-start | bytes 292
  148.3 20.4 %all-to-all-start.2 = ((bf16[8,2,4,3,8,128]{5,4,3,2,1,0:T(8,128)(2,1)}), bf16[8,2,4,3,8,128]{5,4,3,2,1,0:T(8,128)(2,1)}, u32[]{:S(2)}, u32[]{:S(2)}) async-start(bf16[8,2,4,3,8,128]{5,4,3,2,1,0:T(8,128)(2,1)} %bitcast.251), calls=%async_computation.3 | async-start | bytes 786432 | tf_op jit(solution)/shard_map/all_to_all | solution.py:130
  182.1 26.6 %all-to-all-start.6 = ((bf16[8,24,256]{2,1,0:T(8,128)(2,1)}), bf16[8,24,256]{2,1,0:T(8,128)(2,1)}, u32[]{:S(2)}, u32[]{:S(2)}) async-start(bf16[8,24,256]{2,1,0:T(8,128)(2,1)} %copy.339), calls=%async_computation.7 | async-start | bytes 196608 | tf_op jit(solution)/shard_map/all_to_all | solution.py:214
  188.9 14.3 %copy-start.30 = (f32[192,512]{1,0:T(8,128)S(1)}, f32[192,512]{1,0:T(8,128)}, u32[]{:S(2)}) copy-start(f32[192,512]{1,0:T(8,128)} %copy-done.29) | copy-start | bytes 1179652
  188.9 15.0 %copy-start.11 = (bf16[1024,512]{1,0:T(8,128)(2,1)S(1)}, bf16[1024,512]{1,0:T(8,128)(2,1)}, u32[]{:S(2)}) copy-start(bf16[1024,512]{1,0:T(8,128)(2,1)} %param.31) | copy-start | bytes 3145732
  193.1 13.6 %copy-start.44 = (f32[192]{0:T(256)S(1)}, f32[192]{0:T(256)}, u32[]{:S(2)}) copy-start(f32[192]{0:T(256)} %copy-done.43) | copy-start | bytes 2308
  193.1 13.6 %copy-start.46 = (f32[1024]{0:T(1024)S(1)}, f32[1024]{0:T(1024)}, u32[]{:S(2)}) copy-start(f32[1024]{0:T(1024)} %param.30) | copy-start | bytes 12292
  193.1 13.6 %copy-start.50 = (f32[192]{0:T(256)S(1)}, f32[192]{0:T(256)}, u32[]{:S(2)}) copy-start(f32[192]{0:T(256)} %copy-done.49) | copy-start | bytes 2308
  203.9 16.7 %copy-start.58 = (f32[24]{0:T(128)S(1)}, f32[24]{0:T(128)}, u32[]{:S(2)}) copy-start(f32[24]{0:T(128)} %copy-done.57) | copy-start | bytes 292
  203.9 16.6 %copy-start.65 = (f32[24]{0:T(128)S(1)}, f32[24]{0:T(128)}, u32[]{:S(2)}) copy-start(f32[24]{0:T(128)} %add_rsqrt_fusion.5) | copy-start | bytes 292
  205.2 25.2 %copy-start.17 = (bf16[128,1024]{1,0:T(8,128)(2,1)S(1)}, bf16[128,1024]{1,0:T(8,128)(2,1)}, u32[]{:S(2)}) copy-start(bf16[128,1024]{1,0:T(8,128)(2,1)} %param.28) | copy-start | bytes 786436
  205.2 25.3 %copy-start.31 = (f32[192,128]{1,0:T(8,128)S(1)}, f32[192,128]{1,0:T(8,128)}, u32[]{:S(2)}) copy-start(f32[192,128]{1,0:T(8,128)} %copy.324) | copy-start | bytes 294916
  208.7 11.7 %all-to-all-start.3 = ((bf16[8,24,1024]{2,1,0:T(8,128)(2,1)}), bf16[8,24,1024]{2,1,0:T(8,128)(2,1)S(1)}, u32[]{:S(2)}, u32[]{:S(2)}) async-start(bf16[8,24,1024]{2,1,0:T(8,128)(2,1)} %bitcast.44), calls=%async_computation.4 | async-start | bytes 786432 | tf_op jit(solution)/shard_map/all_to_all | solution.py:186
  230.4 35.2 %copy-start.12 = (bf16[192,1024]{1,0:T(8,128)(2,1)}, bf16[192,1024]{1,0:T(8,128)(2,1)S(1)}, u32[]{:S(2)}) copy-start(bf16[192,1024]{1,0:T(8,128)(2,1)S(1)} %all_gather.58) | copy-start | bytes 1179652
  271.4 9.1 %collective-permute-start.2 = (bf16[768,128]{1,0:T(8,128)(2,1)}, bf16[768,128]{1,0:T(8,128)(2,1)S(1)}, u32[]{:S(2)}, u32[]{:S(2)}) collective-permute-start(bf16[768,128]{1,0:T(8,128)(2,1)} %reshape_reshape.15), channel_id=1, source_target_pairs={{0,8},{8,0},{16,24},{24,16},{1,9},{9,1},{17,25},{25,17},{2,10},{10... | collective-permute-start | bytes 589832 | tf_op jit(solution)/shard_map/ppermute | solution.py:46
  282.2 8.7 %collective-permute-start.3 = (bf16[768,128]{1,0:T(8,128)(2,1)S(1)}, bf16[768,128]{1,0:T(8,128)(2,1)S(1)}, u32[]{:S(2)}, u32[]{:S(2)}) collective-permute-start(bf16[768,128]{1,0:T(8,128)(2,1)S(1)} %add.309), channel_id=1, source_target_pairs={{0,16},{8,24},{16,0},{24,8},{1,17},{9,25},{17,1},{25,9},{2,18},{10... | collective-permute-start | bytes 589832 | tf_op jit(solution)/shard_map/ppermute | solution.py:46
  298.9 7.4 %collective-permute-start.4 = (f32[8512]{0:T(1024)S(1)}, f32[8512]{0:T(1024)S(1)}, u32[]{:S(2)}, u32[]{:S(2)}) collective-permute-start(f32[8512]{0:T(1024)S(1)} %concatenate.55), channel_id=1, source_target_pairs={{0,1},{1,0},{2,3},{3,2},{4,5},{5,4},{6,7},{7,6},{8,9},{9,8},{10,11... | collective-permute-start | bytes 102152 | tf_op jit(solution)/shard_map/ppermute | solution.py:46
  298.9 9.3 %copy-start.13 = (bf16[192,1024]{1,0:T(8,128)(2,1)S(1)}, bf16[192,1024]{1,0:T(8,128)(2,1)}, u32[]{:S(2)}) copy-start(bf16[192,1024]{1,0:T(8,128)(2,1)} %copy-done.12) | copy-start | bytes 1179652
  301.6 26.7 %copy-start.60 = (f32[2,128]{1,0:T(2,128)S(1)}, f32[2,128]{1,0:T(2,128)}, u32[]{:S(2)}) copy-start(f32[2,128]{1,0:T(2,128)} %fusion.75) | copy-start | bytes 3076
  301.6 29.2 %copy-start.48 = (f32[2,4,3]{2,1,0:T(4,128)S(1)}, f32[2,4,3]{2,1,0:T(4,128)}, u32[]{:S(2)}) copy-start(f32[2,4,3]{2,1,0:T(4,128)} %get-tuple-element.176) | copy-start | bytes 292
  301.6 29.2 %copy-start.56 = (f32[2,4]{1,0:T(2,128)S(1)}, f32[2,4]{1,0:T(2,128)}, u32[]{:S(2)}) copy-start(f32[2,4]{1,0:T(2,128)} %copy-done.55) | copy-start | bytes 100
  301.6 49.1 %all-to-all-start.5 = ((bf16[8,2,96,512]{3,2,1,0:T(8,128)(2,1)}), bf16[8,2,96,512]{3,2,1,0:T(8,128)(2,1)}, u32[]{:S(2)}, u32[]{:S(2)}) async-start(bf16[8,2,96,512]{3,2,1,0:T(8,128)(2,1)} %copy.333), calls=%async_computation.6 | async-start | bytes 3145728 | tf_op jit(solution)/shard_map/all_to_all | solution.py:286
  306.0 145.6 %all-reduce.5.cloned.1.call-start = ((), (), s32[]{:S(2)}) async-start(), calls=%async_computation.12 | async-start | bytes 7340032 | tf_op jit(solution)/shard_map/psum | solution.py:301
  306.3 20.5 %collective-permute-start.5 = (f32[8512]{0:T(1024)S(1)}, f32[8512]{0:T(1024)S(1)}, u32[]{:S(2)}, u32[]{:S(2)}) collective-permute-start(f32[8512]{0:T(1024)S(1)} %add.314), channel_id=1, source_target_pairs={{0,2},{1,3},{2,0},{3,1},{4,6},{5,7},{6,4},{7,5},{8,10},{9,11},{10,... | collective-permute-start | bytes 102152 | tf_op jit(solution)/shard_map/ppermute | solution.py:46
  326.8 4.0 collective-permute-start.6
  330.8 6.4 %collective-permute-start.7 = (f32[8512]{0:T(1024)S(1)}, f32[8512]{0:T(1024)S(1)}, u32[]{:S(2)}, u32[]{:S(2)}) collective-permute-start(f32[8512]{0:T(1024)S(1)} %add.316), channel_id=1, source_target_pairs={{0,8},{8,0},{16,24},{24,16},{1,9},{9,1},{17,25},{25,17},{2,10},{10... | collective-permute-start | bytes 102152 | tf_op jit(solution)/shard_map/ppermute | solution.py:46
  337.1 17.1 %copy-start.52 = (f32[2,96]{1,0:T(2,128)S(1)}, f32[2,96]{1,0:T(2,128)}, u32[]{:S(2)}) copy-start(f32[2,96]{1,0:T(2,128)} %copy-done.51) | copy-start | bytes 2308
  337.2 17.1 %copy-start.59 = (f32[2,96]{1,0:T(2,128)S(1)}, f32[2,96]{1,0:T(2,128)}, u32[]{:S(2)}) copy-start(f32[2,96]{1,0:T(2,128)} %add_rsqrt_fusion.2) | copy-start | bytes 2308
  337.2 8.3 %collective-permute-start.8 = (f32[8512]{0:T(1024)S(1)}, f32[8512]{0:T(1024)S(1)}, u32[]{:S(2)}, u32[]{:S(2)}) collective-permute-start(f32[8512]{0:T(1024)S(1)} %add.317), channel_id=1, source_target_pairs={{0,16},{8,24},{16,0},{24,8},{1,17},{9,25},{17,1},{25,9},{2,18},{10... | collective-permute-start | bytes 102152 | tf_op jit(solution)/shard_map/ppermute | solution.py:46
  350.7 18.9 %all-to-all-start.4 = ((bf16[8,2,128,256]{3,2,1,0:T(8,128)(2,1)}), bf16[8,2,128,256]{3,2,1,0:T(8,128)(2,1)S(1)}, u32[]{:S(2)}, u32[]{:S(2)}) async-start(bf16[8,2,128,256]{3,2,1,0:T(8,128)(2,1)} %bitcast.56), calls=%async_computation.5 | async-start | bytes 2097152 | tf_op jit(solution)/shard_map/all_to_all | solution.py:283
  354.3 15.3 %copy-start.54 = (f32[2,128]{1,0:T(2,128)S(1)}, f32[2,128]{1,0:T(2,128)}, u32[]{:S(2)}) copy-start(f32[2,128]{1,0:T(2,128)} %copy-done.53) | copy-start | bytes 3076
  (43 other events, 208.9 us)
Sparse Core Ops, SparseCore 0:
  30.2 44.7 reduce-scatter.1
  310.8 140.7 all-reduce.4
Sparse Core Ops, SparseCore 1:
  32.5 28.7 all-gather.11
  63.5 36.8 all-gather.13
  102.7 50.5 all-gather.15
